TPU v7x, 256 devices: a whole 4x4x8 slice. The times are simulated.
256 devices in a mesh: pair: 2 (over core), rep: 32 (over z, x), slab: 4 (over y).
Axes of the slice: x: 4, y: 4, z: 8, core: 2. Of those that a mesh axis runs over, the one named last changes fastest.
Arguments:
- amplitudes: bfloat16 [16384, 4096], P(('pair', 'slab'), 'rep'), may hold values from -6 to 6
- tile_pairs: int32 [16384], P(('pair', 'slab')), may hold values from 0 to 15, as said below
- row_pairs: int32 [16384], P(('pair', 'slab')), may hold values from 0 to 255
- owner: int32 [16], replicated, may hold values from 0 to 15, as said below
- integrals: bfloat16 [2, 16, 4096, 4096], P(None, 'pair', 'rep', 'slab'), may hold values from -0.0625 to 0.0625
Outputs:
- ladder: bfloat16 [2048, 2, 4096], P(('pair', 'slab'), None, 'rep')
Inputs may be any that keep to these rules, and one draw needn't show every extreme that they name: Each occupied pair of a device is named by exactly 8 of its rows, with distinct tile pairs. Call slots p * 8 to (p + 1) * 8 - 1 owner block p. At most 6 tiles of one occupied pair have slots owner[tile_pairs] in one owner block; in the rows of one device at most 1536 do, and every device reaches 1536 for some block. `owner`: each value once.
All inputs are finite; a program needn't handle non-finite values.
Results may differ from a plain program's by a relative error of at most 0.001.
Values may be sent and summed in bfloat16 or wider, within the bound.
No kernel may reach another device: no remote copies, remote signals or barrier semaphores. Data moves between devices by JAX's collectives and lax.ppermute only.
A program may use at most 128 MiB of HBM per device.

v0:
```python
import jax
import jax.numpy as jnp
from jax import lax
from jax.sharding import PartitionSpec as P

PAIRS_DEV = 256


def body(amplitudes, tile_pairs, row_pairs, owner, integrals):
    groups = lax.axis_size("pair")
    tile_count = owner.shape[0]
    slot_width = tile_count // groups
    part_width = amplitudes.shape[1]
    lookup = tile_pairs[:, None] == jnp.arange(tile_count, dtype=jnp.int32)[None, :]
    slots = jnp.sum(jnp.where(lookup, owner[None, :], 0), axis=1)
    target = slots // slot_width
    local_slot = slots % slot_width
    place = (target * PAIRS_DEV + row_pairs) * slot_width + local_slot
    sendbuf = (
        jnp.zeros((groups * PAIRS_DEV * slot_width, part_width), jnp.bfloat16)
        .at[place]
        .set(amplitudes)
    )
    received = lax.all_to_all(
        sendbuf.reshape(groups, PAIRS_DEV * slot_width, part_width),
        "pair",
        split_axis=0,
        concat_axis=0,
        tiled=True,
    )
    operand = received.reshape(groups * PAIRS_DEV, slot_width * part_width)
    piece = lax.all_gather(integrals, "slab", axis=3, tiled=True)
    flat_piece = piece.reshape(piece.shape[0], -1, piece.shape[3])
    products = jnp.einsum("rk,ckn->rcn", operand, flat_piece, preferred_element_type=jnp.float32)
    partial_sum = lax.psum_scatter(products, "rep", scatter_dimension=2, tiled=True)
    result = lax.psum_scatter(partial_sum, "pair", scatter_dimension=0, tiled=True)
    return result.astype(jnp.bfloat16)


def solution(mesh):
    return jax.shard_map(
        body,
        mesh=mesh,
        in_specs=(
            P(("pair", "slab"), "rep"),
            P(("pair", "slab")),
            P(("pair", "slab")),
            P(),
            P(None, "pair", "rep", "slab"),
        ),
        out_specs=P(("pair", "slab"), None, "rep"),
        check_vma=False,
    )
```

profile of v0, /device:TPU:1, one launch (start us, length us, event | category | flops | bytes accessed | tf_op | source)
XLA Modules:
  0.0 454.6 jit_solution(795973035956883995)
XLA Ops:
  6.5 0.0 all-gather.2.cloned.1.call-start
  6.5 0.7 all-gather.2.cloned.1.call-update
  7.3 0.0 reduce-scatter.3.cloned.1.call-start
  7.3 0.8 select_reduce_fusion
  8.1 0.7 compare_select_fusion
  8.8 6.4 %scatter_custom_fusion = bf16[4096,128]{1,0:T(8,128)(2,1)S(1)} fusion(s32[2048]{0:T(1024)S(1)} %compare_select_fusion, bf16[2048,128]{1,0:T(8,128)(2,1)} %param.5, bf16[]{:T(256)} %constant.28.clone.1), kind=kCustom, calls=%fused_computation.1 | custom fusion | bytes 1049088 | tf_op jit(solution)/shard_map/scatter | solution.py:22
  15.2 7.4 %all_to_all.5 = bf16[2,2048,128]{2,1,0:T(8,128)(2,1)S(1)} all-to-all(bf16[2,2048,128]{2,1,0:T(8,128)(2,1)S(1)} %bitcast.5), channel_id=1, replica_groups=mesh['pair'=2,'rep'=32,'slab'=4] {'pair'}, dimensions={0} | all-to-all | bytes 2097152 | tf_op jit(solution)/shard_map/all_to_all | solution.py:24
  22.7 0.5 reshape.23
  23.2 146.4 %all-gather.2.cloned.1.call-done = bf16[2,8,128,4096]{3,2,1,0:T(8,128)(2,1)} async-done(((bf16[2,8,128,1024]{3,2,1,0:T(8,128)(2,1)}), bf16[2,8,128,4096]{3,2,1,0:T(8,128)(2,1)}) %all-gather.2.cloned.1.call-update) | async-done | bytes 16777232 | tf_op jit(solution)/shard_map/all_gather | solution.py:32
  169.6 15.6 %fusion.10 = f32[512,2,4096]{2,0,1:T(8,128)} fusion(bf16[512,1024,1]{1,0,2:T(8,128)(2,1)S(1)} %reshape.23, bf16[2,1024,4096]{2,1,0:T(8,128)(2,1)} %bitcast.6), kind=kOutput, calls=%fused_computation.20 | convolution fusion | flops 8589934592 | bytes 34603008 | tf_op jit(solution)/shard_map/rk,ckn->rcn/dot_general | solution.py:34
  185.2 0.0 reduce-scatter.3.cloned.1.call-update
  185.2 0.0 reduce-scatter.5.cloned.1.call-start
  185.3 242.3 %reduce-scatter.3.cloned.1.call-done = f32[512,2,128]{2,0,1:T(8,128)} async-done(((f32[512,2,4096]{2,0,1:T(8,128)}), f32[512,2,128]{2,0,1:T(8,128)}) %reduce-scatter.3.cloned.1.call-update) | async-done | bytes 524304 | tf_op jit(solution)/shard_map/reduce_scatter | solution.py:35
  427.6 0.0 reduce-scatter.5.cloned.1.call-update
  427.6 18.7 %reduce-scatter.5.cloned.1.call-done = f32[256,2,128]{2,0,1:T(8,128)} async-done(((f32[512,2,128]{2,0,1:T(8,128)}), f32[256,2,128]{2,0,1:T(8,128)}) %reduce-scatter.5.cloned.1.call-update) | async-done | bytes 262160 | tf_op jit(solution)/shard_map/reduce_scatter | solution.py:36
  446.3 1.0 convert_element_type.3
  447.2 0.8 copy.8
Async XLA Ops:
  6.5 163.1 %all-gather.2.cloned.1.call-start = ((), (), s32[]{:S(2)}) async-start(), calls=%async_computation.3 | async-start | bytes 20971520 | tf_op jit(solution)/shard_map/all_gather | solution.py:32
  7.3 420.3 %reduce-scatter.3.cloned.1.call-start = ((), (), s32[]{:S(2)}) async-start(), calls=%async_computation.4 | async-start | bytes 17301504 | tf_op jit(solution)/shard_map/reduce_scatter | solution.py:35
  185.2 261.0 %reduce-scatter.5.cloned.1.call-start = ((), (), s32[]{:S(2)}) async-start(), calls=%async_computation.5 | async-start | bytes 786432 | tf_op jit(solution)/shard_map/reduce_scatter | solution.py:36
Sparse Core Ops, SparseCore 0:
  9.2 160.4 all-gather.1
  185.4 242.1 reduce-scatter.2
  430.1 16.1 reduce-scatter.4
where the time goes:
time: 455 us
  waiting for transfers between devices  408 us (90%)
  matrix products  15.6 us (3%)
  between operations  13.1 us (3%)
  local copies, waits for them, and re-layouts  7.67 us (2%)
  blocking collectives  7.44 us (2%)
    reduce_scatter x1, waiting for transfers between devices, body(): lax.psum_scatter(products, 'rep', scatter_dimension=2, tiled=True)  242 us
    all_gather x1, waiting for transfers between devices, body(): piece = lax.all_gather(integrals, 'slab', axis=3, tiled=True)  146 us
    reduce_scatter x1, waiting for transfers between devices, body(): lax.psum_scatter(partial_sum, 'pair', scatter_dimension=0, tiled=True)  18.7 us
    dot_general x1, matrix products, body(): jnp.einsum('rk,ckn->rcn', operand, flat_piece, preferred_element_type=jnp...  15.6 us
  transfers between devices with their start and end apart: 3, of which 3 were waited for; matrix products, arithmetic and copies ran while one was open for 2% of the time, Pallas kernels for 0%

commit v1 on v0

--- a/solution.py
+++ b/solution.py
@@ -29,7 +29,8 @@
         tiled=True,
     )
     operand = received.reshape(groups * PAIRS_DEV, slot_width * part_width)
-    piece = lax.all_gather(integrals, "slab", axis=3, tiled=True)
+    repeated = jnp.stack([integrals] * lax.axis_size("slab"))
+    piece = jnp.concatenate(lax.all_to_all(repeated, "slab", 0, 0), axis=3)
     flat_piece = piece.reshape(piece.shape[0], -1, piece.shape[3])
     products = jnp.einsum("rk,ckn->rcn", operand, flat_piece, preferred_element_type=jnp.float32)
     partial_sum = lax.psum_scatter(products, "rep", scatter_dimension=2, tiled=True)

time: 455 us -> 556 us (1.22)
  local copies, waits for them, and re-layouts: 7.67 us -> 64.9 us
  waiting for transfers between devices: 408 us -> 444 us
  starting transfers between devices: 0.08 us -> 7.04 us
    all_to_all x0 -> x1, waiting for transfers between devices: none -> 183 us  [body(): piece = jnp.concatenate(lax.all_to_all(repeated, 'slab', 0, 0), axis=3)]
    all_gather x1 -> x0, waiting for transfers between devices: 146 us -> none  [body(): piece = lax.all_gather(integrals, 'slab', axis=3, tiled=True)]
    another operation x0 -> x2, local copies, waits for them, and re-layouts: none -> 35 us  [the longest x1 27.6 us: body(): flat_piece = piece.reshape(piece.shape[0], -1, piece.shape[3])]
    reshape x0 -> x1, local copies, waits for them, and re-layouts: none -> 22.2 us  [body(): piece = jnp.concatenate(lax.all_to_all(repeated, 'slab', 0, 0), axis=3)]
    all_to_all x0 -> x1, starting transfers between devices: none -> 6.96 us  [body(): piece = jnp.concatenate(lax.all_to_all(repeated, 'slab', 0, 0), axis=3)]
  transfers between devices with their start and end apart: 3 -> 3, of which waited for: 3 -> 3; matrix products, arithmetic and copies ran while one was open for 2% -> 0% of each run, Pallas kernels for 0% -> 0%
where the time goes in v1:
time: 556 us; the launch traced here: 555 us
  waiting for transfers between devices  444 us (80%)
  local copies, waits for them, and re-layouts  64.9 us (12%)
  matrix products  15.6 us (3%)
  between operations  13.4 us (2%)
  blocking collectives  7.44 us (1%)
  starting transfers between devices  7.04 us (1%)
    reduce_scatter x1, waiting for transfers between devices, body(): lax.psum_scatter(products, 'rep', scatter_dimension=2, tiled=True)  242 us
    all_to_all x1, waiting for transfers between devices, body(): piece = jnp.concatenate(lax.all_to_all(repeated, 'slab', 0, 0), axis=3)  183 us
    another operation x1, local copies, waits for them, and re-layouts, body(): flat_piece = piece.reshape(piece.shape[0], -1, piece.shape[3])  27.6 us
    reshape x1, local copies, waits for them, and re-layouts, body(): piece = jnp.concatenate(lax.all_to_all(repeated, 'slab', 0, 0), axis=3)  22.2 us
    reduce_scatter x1, waiting for transfers between devices, body(): lax.psum_scatter(partial_sum, 'pair', scatter_dimension=0, tiled=True)  19 us
    dot_general x1, matrix products, body(): jnp.einsum('rk,ckn->rcn', operand, flat_piece, preferred_element_type=jnp...  15.6 us
  transfers between devices with their start and end apart: 3, of which 3 were waited for; matrix products, arithmetic and copies ran while one was open for 0% of the time, Pallas kernels for 0%

profile of v1, /device:TPU:1, one launch (start us, length us, event | category | flops | bytes accessed | tf_op | source)
XLA Modules:
  0.0 554.6 jit_solution(14287037318151042676)
XLA Ops:
  6.5 0.8 select_reduce_fusion
  7.3 0.7 compare_select_fusion
  8.1 6.4 %scatter_custom_fusion = bf16[4096,128]{1,0:T(8,128)(2,1)S(1)} fusion(s32[2048]{0:T(1024)S(1)} %compare_select_fusion, bf16[2048,128]{1,0:T(8,128)(2,1)} %param.5, bf16[]{:T(256)} %constant.28.clone.1), kind=kCustom, calls=%fused_computation.1 | custom fusion | bytes 1049088 | tf_op jit(solution)/shard_map/scatter | solution.py:22
  14.5 7.4 %all_to_all.10 = bf16[2,2048,128]{2,1,0:T(8,128)(2,1)S(1)} all-to-all(bf16[2,2048,128]{2,1,0:T(8,128)(2,1)S(1)} %bitcast.4), channel_id=1, replica_groups=mesh['pair'=2,'rep'=32,'slab'=4] {'pair'}, dimensions={0} | all-to-all | bytes 2097152 | tf_op jit(solution)/shard_map/all_to_all | solution.py:24
  21.9 7.5 %stack.2 = bf16[4,2,8,128,1024]{4,3,2,1,0:T(8,128)(2,1)} broadcast(bf16[2,8,128,1024]{3,2,1,0:T(8,128)(2,1)} %param.9), dimensions={1,2,3,4} | broadcast | bytes 20971520 | tf_op jit(solution)/shard_map/stack | solution.py:32
  29.4 7.0 %all-to-all-start.1 = ((bf16[4,2,8,128,1024]{4,3,2,1,0:T(8,128)(2,1)}), bf16[4,2,8,128,1024]{4,3,2,1,0:T(8,128)(2,1)}, u32[]{:S(2)}, u32[]{:S(2)}) async-start(bf16[4,2,8,128,1024]{4,3,2,1,0:T(8,128)(2,1)} %stack.2), calls=%async_computation.1 | async-start | bytes 33554432 | tf_op jit(solution)/shard_map/all_to_all | solution.py:33
  36.3 0.0 reduce-scatter.3.cloned.1.call-start
  36.4 0.5 reshape.25
  36.9 182.9 %all-to-all-done.1 = bf16[4,2,8,128,1024]{4,3,2,1,0:T(8,128)(2,1)} async-done(((bf16[4,2,8,128,1024]{4,3,2,1,0:T(8,128)(2,1)}), bf16[4,2,8,128,1024]{4,3,2,1,0:T(8,128)(2,1)}, u32[]{:S(2)}, u32[]{:S(2)}) %all-to-all-start.1) | async-done | bytes 16777248 | tf_op jit(solution)/shard_map/all_to_all | solution.py:33
  219.8 22.2 %copy.10 = bf16[2,8,128,4,1024]{4,3,2,1,0:T(4,128)(2,1)} copy(bf16[2,8,128,4,1024]{4,2,1,0,3:T(8,128)(2,1)} %bitcast.1) | data formatting | bytes 33554432 | tf_op jit(solution)/shard_map/reshape | solution.py:33
  242.0 27.6 %reshape_reshape.3 = bf16[2,1024,4096]{2,1,0:T(8,128)(2,1)} reshape(bf16[2,8,128,4,1024]{4,3,2,1,0:T(4,128)(2,1)} %copy.10) | data formatting | bytes 33554432 | tf_op jit(solution)/shard_map/reshape;reshape | solution.py:34
  269.5 15.6 %fusion.10 = f32[512,2,4096]{2,0,1:T(8,128)} fusion(bf16[512,1024,1]{1,0,2:T(8,128)(2,1)S(1)} %reshape.25, bf16[2,1024,4096]{2,1,0:T(8,128)(2,1)} %reshape_reshape.3), kind=kOutput, calls=%fused_computation.20 | convolution fusion | flops 8589934592 | bytes 34603008 | tf_op jit(solution)/shard_map/rk,ckn->rcn/dot_general | solution.py:35
  285.1 0.0 reduce-scatter.3.cloned.1.call-update
  285.2 0.0 reduce-scatter.5.cloned.1.call-start
  285.2 241.7 %reduce-scatter.3.cloned.1.call-done = f32[512,2,128]{2,0,1:T(8,128)} async-done(((f32[512,2,4096]{2,0,1:T(8,128)}), f32[512,2,128]{2,0,1:T(8,128)}) %reduce-scatter.3.cloned.1.call-update) | async-done | bytes 524304 | tf_op jit(solution)/shard_map/reduce_scatter | solution.py:36
  526.9 0.0 reduce-scatter.5.cloned.1.call-update
  526.9 19.0 %reduce-scatter.5.cloned.1.call-done = f32[256,2,128]{2,0,1:T(8,128)} async-done(((f32[512,2,128]{2,0,1:T(8,128)}), f32[256,2,128]{2,0,1:T(8,128)}) %reduce-scatter.5.cloned.1.call-update) | async-done | bytes 262160 | tf_op jit(solution)/shard_map/reduce_scatter | solution.py:37
  546.0 1.0 convert_element_type.3
  546.9 0.8 copy.11
Async XLA Ops:
  29.4 190.4 %all-to-all-start.1 = ((bf16[4,2,8,128,1024]{4,3,2,1,0:T(8,128)(2,1)}), bf16[4,2,8,128,1024]{4,3,2,1,0:T(8,128)(2,1)}, u32[]{:S(2)}, u32[]{:S(2)}) async-start(bf16[4,2,8,128,1024]{4,3,2,1,0:T(8,128)(2,1)} %stack.2), calls=%async_computation.1 | async-start | bytes 33554432 | tf_op jit(solution)/shard_map/all_to_all | solution.py:33
  36.3 490.5 %reduce-scatter.3.cloned.1.call-start = ((), (), s32[]{:S(2)}) async-start(), calls=%async_computation.4 | async-start | bytes 17301504 | tf_op jit(solution)/shard_map/reduce_scatter | solution.py:36
  285.2 260.8 %reduce-scatter.5.cloned.1.call-start = ((), (), s32[]{:S(2)}) async-start(), calls=%async_computation.5 | async-start | bytes 786432 | tf_op jit(solution)/shard_map/reduce_scatter | solution.py:37
Sparse Core Ops, SparseCore 0:
  285.3 241.5 reduce-scatter.2
  529.4 16.5 reduce-scatter.4
